TPU v7x, 32 devices: a whole 2x2x4 slice. The times are simulated.
32 devices in a mesh: layer: 2 (over y), rows: 16 (over z, x, core).
Axes of the slice: x: 2, y: 2, z: 4, core: 2. Of those that a mesh axis runs over, the one named last changes fastest.
Arguments:
- weights: bfloat16 [2, 3712, 8192], P('layer', 'rows'), may hold values from -150 to 150
- sketch: bfloat16 [8192, 128], P('rows'), may hold values from -6 to 6
Outputs:
- base: bfloat16 [3712, 8192], P('rows', 'layer')
- range_basis: float32 [2, 3712, 128], P('layer', 'rows')
- lora_left: float32 [2, 3712, 128], P('layer', 'rows')
- lora_right: float32 [2, 8192, 128], P('layer', 'rows')
All inputs are finite; a program needn't handle non-finite values.
Results may differ from a plain program's by a relative error of at most 0.002.
The roundings to bfloat16 on the way count: a program that leaves them out, or rounds other values in their place, can miss the bound.
Values may be sent and summed in bfloat16 or wider, within the bound.
A program may use at most 64 MiB of HBM per device.

v0:
```python
import math

import jax
import jax.numpy as jnp
from jax import lax
from jax.sharding import PartitionSpec as P


def full_dot(left_side, right_side):
    return jnp.dot(
        left_side, right_side, precision=lax.Precision.HIGHEST, preferred_element_type=jnp.float32
    )


def shards(weights, sketch):
    layer_w = weights[0]
    hidden_rows, model_width = layer_w.shape
    layers = lax.axis_size("layer")
    block_width = model_width // layers
    layer_total = lax.psum(layer_w, "layer").astype(jnp.float32)
    base_full = (layer_total / layers).astype(jnp.bfloat16)
    residual = layer_w.astype(jnp.float32) - base_full.astype(jnp.float32)
    base_part = lax.dynamic_slice_in_dim(
        base_full, lax.axis_index("layer") * block_width, block_width, 1
    )
    columns = residual
    sampled = full_dot(
        columns, lax.all_gather(sketch, "rows", axis=0, tiled=True).astype(jnp.float32)
    )
    gram_y = lax.psum(full_dot(sampled.T, sampled), "rows")
    lower_tri = jnp.linalg.cholesky(gram_y)
    range_basis = jax.scipy.linalg.solve_triangular(lower_tri, sampled.T, lower=True).T
    columns = residual
    co_part = lax.psum_scatter(
        full_dot(columns.T, range_basis), "rows", scatter_dimension=0, tiled=True
    )
    gram_z = lax.psum(full_dot(co_part.T, co_part), "rows")
    columns = residual
    projected = full_dot(
        columns,
        lax.all_gather(co_part.astype(jnp.bfloat16), "rows", axis=0, tiled=True).astype(
            jnp.float32
        ),
    )
    lower_row = jnp.linalg.cholesky(gram_z)
    left_factor = jax.scipy.linalg.solve_triangular(lower_row, projected.T, lower=True).T
    right_factor = (
        math.sqrt(model_width)
        * jax.scipy.linalg.solve_triangular(lower_row, co_part.T, lower=True).T
    )
    return (base_part, range_basis[None], left_factor[None], right_factor[None])


def solution(mesh):
    placed = (P("layer", "rows", None), P("rows", None))
    return jax.shard_map(
        shards,
        mesh=mesh,
        in_specs=placed,
        out_specs=(
            P("rows", "layer"),
            P("layer", "rows", None),
            P("layer", "rows", None),
            P("layer", "rows", None),
        ),
        check_vma=False,
    )
```

profile of v0, /device:TPU:0, one launch (start us, length us, event | category | flops | bytes accessed | tf_op | source)
XLA Modules:
  0.0 473.7 jit_solution(15090191845868666787)
XLA Ops:
  8.0 0.0 all-reduce.4.cloned.1.call-start
  8.0 0.7 all-reduce.4.cloned.1.call-update
  8.7 0.0 all-gather.3.cloned.1.call-start
  8.8 0.5 all-gather.3.cloned.1.call-update
  9.3 0.0 all-reduce.6.cloned.1.call-start
  9.4 104.5 %all-reduce.4.cloned.1.call-done = bf16[232,8192]{1,0:T(8,128)(2,1)} async-done(((bf16[232,8192]{1,0:T(8,128)(2,1)}), bf16[232,8192]{1,0:T(8,128)(2,1)}) %all-reduce.4.cloned.1.call-update) | async-done | bytes 3801104 | tf_op jit(solution)/shard_map/psum | solution.py:20
  113.9 0.0 all-gather.3.cloned.1.call-done
  113.9 7.7 %fusion.2 = f32[232,128]{1,0:T(8,128)S(1)} fusion(bf16[8192,128]{1,0:T(8,128)(2,1)} %all-gather.3.cloned.1.call-done, bf16[1,232,8192]{2,1,0:T(8,128)(2,1)} %param.5, bf16[232,8192]{1,0:T(8,128)(2,1)} %all-reduce.4.cloned.1.call-done), kind=kOutput, calls=%fused_computation.4 | convolution fusion | flops 2930638848 | bytes 9818112 | tf_op jit(solution)/shard_map/dot_general | solution.py:10
  121.6 1.0 fusion.16
  122.6 0.0 all-reduce.6.cloned.1.call-update
  122.7 0.0 reduce-scatter.2.cloned.1.call-start
  122.7 84.3 %all-reduce.6.cloned.1.call-done = f32[128,128]{0,1:T(8,128)} async-done(((f32[128,128]{0,1:T(8,128)}), f32[128,128]{0,1:T(8,128)}) %all-reduce.6.cloned.1.call-update) | async-done | bytes 65552 | tf_op jit(solution)/shard_map/psum | solution.py:30
  207.0 0.9 copy.7
  207.9 0.9 fusion.12
  208.8 11.7 %cholesky.44 = f32[128,128]{1,0:T(8,128)S(1)} custom-call(f32[128,128]{1,0:T(8,128)S(1)} %fusion.12), custom_call_target="Cholesky" | custom-call | tf_op jit(solution)/shard_map/jit(cholesky)/cholesky | solution.py:31
  220.6 0.6 compare_reduce_fusion.1
  221.2 0.7 fusion.6
  221.9 9.8 %custom-call.11 = f32[1,128,128]{1,2,0:T(8,128)S(1)} custom-call(f32[1,128,128]{2,1,0:T(8,128)S(1)} %fusion.6), custom_call_target="InvertDiagBlocksLowerTriangular" | custom-call | tf_op jit(solution)/shard_map/jit(_solve_triangular)/triangular_solve | solution.py:32
  231.7 0.3 fusion.4
  232.0 0.0 copy-start.1
  232.0 17.1 %fusion.1 = f32[8192,128]{1,0:T(8,128)} fusion(f32[128,232]{0,1:T(8,128)S(1)} %fusion.4, bf16[1,232,8192]{2,1,0:T(8,128)(2,1)} %param.5, bf16[232,8192]{1,0:T(8,128)(2,1)} %all-reduce.4.cloned.1.call-done), kind=kOutput, calls=%fused_computation.3 | convolution fusion | flops 2930638848 | bytes 11915264 | tf_op jit(solution)/shard_map/dot_general | solution.py:10
  249.1 0.0 copy-done.1
  249.1 0.0 reduce-scatter.2.cloned.1.call-update
  249.2 0.0 all-reduce.8.cloned.1.call-start
  249.2 73.9 %reduce-scatter.2.cloned.1.call-done = f32[512,128]{1,0:T(8,128)} async-done(((f32[8192,128]{1,0:T(8,128)}), f32[512,128]{1,0:T(8,128)}) %reduce-scatter.2.cloned.1.call-update) | async-done | bytes 262160 | tf_op jit(solution)/shard_map/reduce_scatter | solution.py:34
  323.1 2.2 fusion.17
  325.3 0.0 all-reduce.8.cloned.1.call-update
  325.4 0.3 all-gather.5.cloned.1.call-start
  325.6 1.6 convert_element_type.21
  327.3 0.0 all-gather.5.cloned.1.call-update
  327.3 2.8 multiply_convert_fusion
  330.1 0.0 copy-start
  330.1 1.4 constant_dynamic-slice_fusion
  331.5 79.3 %all-reduce.8.cloned.1.call-done = f32[128,128]{0,1:T(8,128)} async-done(((f32[128,128]{0,1:T(8,128)}), f32[128,128]{0,1:T(8,128)}) %all-reduce.8.cloned.1.call-update) | async-done | bytes 65552 | tf_op jit(solution)/shard_map/psum | solution.py:37
  410.8 0.9 copy.9
  411.7 0.9 fusion.10
  412.6 11.7 %cholesky.55 = f32[128,128]{1,0:T(8,128)S(1)} custom-call(f32[128,128]{1,0:T(8,128)S(1)} %fusion.10), custom_call_target="Cholesky" | custom-call | tf_op jit(solution)/shard_map/jit(cholesky)/cholesky | solution.py:45
  424.3 0.6 compare_reduce_fusion
  425.0 0.7 fusion.7
  425.6 9.8 %custom-call.12 = f32[1,128,128]{1,2,0:T(8,128)S(1)} custom-call(f32[1,128,128]{2,1,0:T(8,128)S(1)} %fusion.7), custom_call_target="InvertDiagBlocksLowerTriangular" | custom-call | tf_op jit(solution)/shard_map/jit(_solve_triangular)/triangular_solve | solution.py:46
  435.4 0.0 copy-done
  435.5 1.1 fusion.3
  436.5 19.8 %all-gather.5.cloned.1.call-done = bf16[8192,128]{1,0:T(8,128)(2,1)} async-done(((bf16[512,128]{1,0:T(8,128)(2,1)}), bf16[8192,128]{1,0:T(8,128)(2,1)}) %all-gather.5.cloned.1.call-update) | async-done | bytes 2097168 | tf_op jit(solution)/shard_map/all_gather | solution.py:41
  456.3 8.7 %fusion = f32[128,232]{1,0:T(8,128)S(1)} fusion(bf16[8192,128]{1,0:T(8,128)(2,1)} %all-gather.5.cloned.1.call-done, bf16[1,232,8192]{2,1,0:T(8,128)(2,1)} %param.5, bf16[232,8192]{1,0:T(8,128)(2,1)} %all-reduce.4.cloned.1.call-done), kind=kOutput, calls=%fused_computation.2 | convolution fusion | flops 2930638848 | bytes 9818112 | tf_op jit(solution)/shard_map/dot_general | solution.py:10
  465.0 1.1 convolution_bitcast_fusion
  (2 shorter events, 0.1 us)
Async XLA Ops:
  8.0 105.9 %all-reduce.4.cloned.1.call-start = ((), (), s32[]{:S(2)}) async-start(), calls=%async_computation.1 | async-start | bytes 7602176 | tf_op jit(solution)/shard_map/psum | solution.py:20
  8.7 105.2 %all-gather.3.cloned.1.call-start = ((), (), s32[]{:S(2)}) async-start(), calls=%async_computation.2 | async-start | bytes 2228224 | tf_op jit(solution)/shard_map/all_gather | solution.py:28
  9.3 197.7 %all-reduce.6.cloned.1.call-start = ((), (), s32[]{:S(2)}) async-start(), calls=%async_computation.3 | async-start | bytes 131072 | tf_op jit(solution)/shard_map/psum | solution.py:30
  122.7 200.4 %reduce-scatter.2.cloned.1.call-start = ((), (), s32[]{:S(2)}) async-start(), calls=%async_computation.4 | async-start | bytes 4456448 | tf_op jit(solution)/shard_map/reduce_scatter | solution.py:34
  232.0 17.1 %copy-start.1 = (f32[128,232]{0,1:T(8,128)}, f32[128,232]{0,1:T(8,128)S(1)}, u32[]{:S(2)}) copy-start(f32[128,232]{0,1:T(8,128)S(1)} %fusion.4) | copy-start | bytes 356356
  249.2 161.6 %all-reduce.8.cloned.1.call-start = ((), (), s32[]{:S(2)}) async-start(), calls=%async_computation.5 | async-start | bytes 131072 | tf_op jit(solution)/shard_map/psum | solution.py:37
  325.4 131.0 %all-gather.5.cloned.1.call-start = ((), (), s32[]{:S(2)}) async-start(), calls=%async_computation.6 | async-start | bytes 2228224 | tf_op jit(solution)/shard_map/all_gather | solution.py:41
  330.1 105.3 %copy-start = (f32[512,128]{1,0:T(8,128)S(1)}, f32[512,128]{1,0:T(8,128)}, u32[]{:S(2)}) copy-start(f32[512,128]{1,0:T(8,128)} %reduce-scatter.2.cloned.1.call-done) | copy-start | bytes 786436
Sparse Core Ops, SparseCore 0:
  11.1 102.7 all-reduce.3
Sparse Core Ops, SparseCore 1:
  11.6 44.1 all-gather.2
  122.8 84.2 all-reduce.5
  249.2 73.8 reduce-scatter.1
  327.6 83.2 all-reduce.7
  413.0 43.3 all-gather.4
where the time goes:
time: 474 us
  waiting for transfers between devices  363 us (77%)
  other arithmetic  51.9 us (11%)
  matrix products  39.2 us (8%)
  between operations  15.8 us (3%)
    psum x1, waiting for transfers between devices, shards(): layer_total = lax.psum(layer_w, 'layer').astype(jnp.float32)  105 us
    psum x1, waiting for transfers between devices, shards(): gram_y = lax.psum(full_dot(sampled.T, sampled), 'rows')  84.3 us
    psum x1, waiting for transfers between devices, shards(): gram_z = lax.psum(full_dot(co_part.T, co_part), 'rows')  79.3 us
    reduce_scatter x1, waiting for transfers between devices, shards(): lax.psum_scatter(full_dot(columns.T, range_basis), 'rows', scatter_dimens...  73.9 us
    dot_general x5, matrix products, full_dot(): jnp.dot(left_side, right_side, precision=lax.Precision.HIGHEST, preferred...  36.7 us
    all_gather x1, waiting for transfers between devices, shards(): lax.all_gather(co_part.astype(jnp.bfloat16), 'rows', axis=0, tiled=True)  19.8 us
    another operation x3, other arithmetic, shards(): lower_row = jnp.linalg.cholesky(gram_z)  12.4 us
    another operation x3, other arithmetic, shards(): lower_tri = jnp.linalg.cholesky(gram_y)  12.4 us
  transfers between devices with their start and end apart: 6, of which 5 were waited for; matrix products, arithmetic and copies ran while one was open for 7% of the time, Pallas kernels for 0%

commit v1 on v0

v1 whole, which is shorter than its diff:
```python
import functools
import math

import jax
import jax.numpy as jnp
from jax import lax
from jax.experimental import pallas as pl
from jax.experimental.pallas import tpu as pltpu
from jax.sharding import PartitionSpec as P

MESH = pl.DeviceIdType.MESH
F32 = jnp.float32
BF16 = jnp.bfloat16
NN = (((1,), (0,)), ((), ()))
NT = (((1,), (1,)), ((), ()))


def flip(value, mask):
    bit = 0
    out = value
    while (1 << bit) <= mask:
        if (mask >> bit) & 1:
            out = out + (1 << bit) * (1 - 2 * ((value // (1 << bit)) % 2))
        bit += 1
    return out


def exact(left, right, dims=NN):
    return lax.dot_general(
        left, right, dims, precision=lax.Precision.HIGHEST, preferred_element_type=F32
    )


def fast(left, right, dims=NN):
    return lax.dot_general(left, right, dims, preferred_element_type=F32)


def split(value):
    high = value.astype(BF16)
    return high, (value - high.astype(F32)).astype(BF16)


def inverse_factor(aug, gram):
    size = gram.shape[0]
    row_of = lax.broadcasted_iota(jnp.int32, (size, size), 0)
    col_of = lax.broadcasted_iota(jnp.int32, (size, size), 1)
    aug[:, :size] = gram
    aug[:, size:] = jnp.where(row_of == col_of, 1.0, 0.0).astype(F32)
    row_id = lax.broadcasted_iota(jnp.int32, (size, 1), 0)
    lane_id = lax.broadcasted_iota(jnp.int32, (1, size), 1)

    def step(k, carry):
        row = aug[pl.ds(k, 1), :]
        left = aug[:, :size]
        right = aug[:, size:]
        hot = lane_id == k
        pivot = jnp.sum(jnp.where(hot, row[:, :size], 0.0), axis=1, keepdims=True)
        scale = lax.rsqrt(pivot)
        scale = scale * (1.5 - 0.5 * (pivot * scale) * scale)
        column = jnp.sum(jnp.where(hot, left, 0.0), axis=1, keepdims=True)
        unit = row * scale
        factor = jnp.where(row_id > k, column * scale, 0.0)
        here = row_id == k
        aug[:, :size] = jnp.where(here, unit[:, :size], left - factor * unit[:, :size])
        aug[:, size:] = jnp.where(here, unit[:, size:], right - factor * unit[:, size:])
        return carry

    lax.fori_loop(0, size, step, 0)
    return aug[:, size:]


def kernel(
    layers, devices,
    w_ref, sketch_ref,
    base_ref, basis_ref, left_ref, right_ref,
    w_in, w_far, e_high, e_low, base_v, s_v,
    y_part, y_in, y_all, p_part, p_in,
    gram, gram_in, inv, w_sum, w_half, z_own, z_recv, z_all,
    h_sum, h_in, h_all, aug,
    local_sem, wy_send, wy_recv, wx_send, wx_recv, s_send, s_recv,
    y_send, y_recv, ya_send, ya_recv, p_send, p_recv,
    g_send, g_recv, l_send, l_recv, ws_send, ws_recv,
    h_send, h_recv, ha_send, ha_recv, za_send, za_recv, zf_send, zf_recv,
):
    h = lax.axis_index("layer")
    r = lax.axis_index("rows")
    n = w_ref.shape[1]
    width = w_ref.shape[2]
    block = width // (2 * layers)
    chunks = devices // (2 * layers)
    x = (r // 2) % 2
    quarter = 2 * h + x
    layer_bits = layers.bit_length() - 1
    row_bits = devices.bit_length() - 1
    bits = [0] + list(range(2, row_bits))
    steps = len(bits)
    pending = []

    def send(src, dst, ss, rs, to_h, to_r):
        copy = pltpu.make_async_remote_copy(
            src_ref=src, dst_ref=dst, send_sem=ss, recv_sem=rs,
            device_id=(to_h, to_r), device_id_type=MESH,
        )
        copy.start()
        pending.append(copy)
        return copy

    barrier = pltpu.get_barrier_semaphore()
    total = layers * devices
    me = h * devices + r

    @pl.loop(1, total)
    def _(i):
        other = lax.rem(me + i, total)
        pl.semaphore_signal(
            barrier, inc=1, device_id=(other // devices, other % devices), device_id_type=MESH
        )

    pl.semaphore_wait(barrier, total - 1)

    def columns(q):
        return pl.ds(pl.multiple_of(q * block, block), block)

    far = []
    near = []
    own_x = flip(r, 2)
    for d in range(1, layers):
        to = flip(h, d)
        far.append(send(w_ref.at[0, :, columns(2 * to + (1 - x))], w_far.at[h],
                        wy_send.at[0, d], wy_recv.at[0, d], to, r))
    for d in range(1, layers):
        to = flip(h, d)
        near.append(send(w_ref.at[0, :, columns(2 * to + x)], w_in.at[h, 0],
                         wy_send.at[1, d], wy_recv.at[1, d], to, r))
    side = [send(w_ref.at[0, :, columns(2 * h + (1 - x))], w_in.at[h, 1],
                 wx_send.at[0], wx_recv.at[0], h, own_x)]
    mine0 = pltpu.make_async_copy(w_ref.at[0, :, columns(quarter)], w_in.at[h, 0], local_sem.at[0])
    mine1 = pltpu.make_async_copy(
        w_ref.at[0, :, columns(2 * h + (1 - x))], w_far.at[h], local_sem.at[1]
    )
    mine0.start()
    mine1.start()

    s_quarter = r // chunks
    s_slot = r % chunks
    sends_s = (s_quarter // 2) == h

    def s_copy(m):
        to = (m // 2) * 4 + (s_quarter % 2) * 2 + m % 2
        return to, pltpu.make_async_remote_copy(
            src_ref=sketch_ref, dst_ref=s_v.at[s_slot], send_sem=s_send.at[m],
            recv_sem=s_recv.at[s_slot], device_id=(h, to), device_id_type=MESH,
        )

    @pl.when(sends_s)
    def _():
        @pl.loop(0, devices // 2)
        def _(m):
            to, copy = s_copy(m)

            @pl.when(to != r)
            def _():
                copy.start()

            @pl.when(to == r)
            def _():
                pltpu.make_async_copy(sketch_ref, s_v.at[s_slot], s_recv.at[s_slot]).start()

    pad = e_high.shape[2]
    if pad > n:
        low = n // 16 * 16
        zero = jnp.zeros((layers, 2, pad - low, block), BF16)
        e_high[:, :, low:, :] = zero
        e_low[:, :, low:, :] = zero

    mine1.wait()
    for d in range(1, layers):
        far[d - 1].wait_recv()
        from_layer = flip(h, d)
        side.append(send(w_far.at[from_layer], w_in.at[from_layer, 1],
                         wx_send.at[d], wx_recv.at[d], h, own_x))

    tile = 128

    @pl.loop(0, block // tile)
    def _(t):
        at = pl.ds(pl.multiple_of(t * tile, tile), tile)
        total_w = w_far[0, :, at].astype(F32)
        for layer in range(1, layers):
            total_w = total_w + w_far[layer, :, at].astype(F32)
        base_v[1, :, at] = (total_w / layers).astype(BF16)

    out1 = pltpu.make_async_copy(base_v.at[1], base_ref.at[:, columns(1 - x)], local_sem.at[2])
    out1.start()

    def residuals(b):
        @pl.loop(0, block // tile)
        def _(t):
            at = pl.ds(pl.multiple_of(t * tile, tile), tile)
            total_w = w_in[0, b, :, at].astype(F32)
            for layer in range(1, layers):
                total_w = total_w + w_in[layer, b, :, at].astype(F32)
            base = (total_w / layers).astype(BF16)
            if b == 0:
                base_v[0, :, at] = base
            base = base.astype(F32)
            for layer in range(layers):
                high, low = split(w_in[layer, b, :, at].astype(F32) - base)
                e_high[layer, b, :n, at] = high
                e_low[layer, b, :n, at] = low

    def sampled(b):
        sketch = s_v[...].reshape(block, s_v.shape[2])
        for layer in range(layers):
            y_part[layer, b] = fast(e_high[layer, b], sketch) + fast(e_low[layer, b], sketch)

    mine0.wait()
    for copy in near:
        copy.wait_recv()
    residuals(0)
    out0 = pltpu.make_async_copy(base_v.at[0], base_ref.at[:, columns(x)], local_sem.at[3])
    out0.start()
    for c in range(chunks):
        pltpu.make_async_copy(sketch_ref, s_v.at[c], s_recv.at[c]).wait()
    sampled(0)
    for copy in side:
        copy.wait_recv()
    residuals(1)
    sampled(1)

    def to_owner(part, slots, ss, rs):
        copies = []
        for d in range(1, 2 * layers):
            to = flip(h, d // 2)
            copies.append(send(part.at[to, d % 2], slots.at[d - 1], ss.at[d], rs.at[d],
                               to, flip(r, 2 * (d % 2))))
        result = part[h, 0]
        for d in range(1, 2 * layers):
            copies[d - 1].wait_recv()
            result = result + slots[d - 1]
        return result

    y_own = to_owner(y_part, y_in, y_send, y_recv)
    y_all[h, 0] = y_own
    copies = []
    for d in range(1, 2 * layers):
        copies.append(send(y_all.at[h, 0], y_all.at[h, d % 2], ya_send.at[d], ya_recv.at[d],
                           flip(h, d // 2), flip(r, 2 * (d % 2))))
    for copy in copies:
        copy.wait_recv()

    def turned(b, layer):
        return y_all[layer, b].T

    def butterfly(total_ref, slots, ss, rs, partners):
        for i, (to_h, to_r) in enumerate(partners):
            copy = send(total_ref.at[i], slots.at[i], ss.at[i], rs.at[i], to_h, to_r)
            copy.wait_recv()
            total_ref[i + 1] = total_ref[i] + slots[i]
        return total_ref[len(partners)]

    gram[0] = exact(turned(0, h), y_all[h, 0]) + exact(turned(1, h), y_all[h, 1])
    g_total = [None]

    piece = width // devices
    for layer in range(layers):
        both = None
        for b in range(2):
            high, low = split(turned(b, layer))
            term = (
                fast(high, e_high[layer, b]) + fast(low, e_high[layer, b])
                + fast(high, e_low[layer, b])
            )
            both = term if both is None else both + term
        for c in range(chunks):
            w_sum[layer * chunks + c] = both[:, c * piece:(c + 1) * piece]

    start = 0
    offset = 0
    length = layers * chunks
    scatter = []
    for s, bit in enumerate(bits):
        half = length // 2
        up = (r // (1 << bit)) % 2
        keep = start + half * up
        give = start + half * (1 - up)
        w_copy = send(w_sum.at[pl.ds(give, half)], w_half.at[pl.ds(offset, half)],
                      ws_send.at[s], ws_recv.at[s], h, flip(r, 1 << bit))
        g_copy = send(gram.at[s], gram_in.at[s], g_send.at[s], g_recv.at[s], h, flip(r, 1 << bit))
        g_copy.wait_recv()
        gram[s + 1] = gram[s] + gram_in[s]
        if s == steps - 1:
            inv[h] = inverse_factor(aug, gram[s + 1])
            l_copies = [
                send(inv.at[h], inv.at[h], l_send.at[d], l_recv.at[d], flip(h, d), r)
                for d in range(1, layers)
            ]
            basis_ref[0] = exact(y_all[h, 0], inv[h], NT)[:n]
        w_copy.wait_recv()

        for i in range(half):
            w_sum[keep + i] = w_sum[keep + i] + w_half[offset + i]
        start = keep
        offset += half
        length = half
    for copy in l_copies:
        copy.wait_recv()

    chunk = start
    layer = chunk // chunks
    z_value = exact(inv[layer], w_sum[chunk])
    z_own[...] = z_value
    z_all[chunk] = z_value.astype(BF16)
    h_sum[0] = exact(z_value, z_value, NT)

    target_h = layer
    target_r = quarter * chunks + chunk % chunks
    stays = (target_h * devices + target_r) == me
    z_move = pltpu.make_async_remote_copy(
        src_ref=z_own, dst_ref=z_recv, send_sem=zf_send.at[0], recv_sem=zf_recv.at[0],
        device_id=(target_h, target_r), device_id_type=MESH,
    )
    z_stay = pltpu.make_async_copy(z_own, z_recv, zf_recv.at[0])

    partners = [(h, flip(r, 2))]
    partners += [(h, flip(r, 1 << bit)) for bit in bits[layer_bits:]]
    partners += [(flip(h, 1 << i), r) for i in range(layer_bits)]
    gather_at = [start]
    length = 1
    last = None
    z_order = list(range(steps))[::-1]
    z_copies = [None] * steps
    z_start = start

    def gather_step(s, z_start, length):
        there = pl.ds(z_start, length)
        return send(z_all.at[there], z_all.at[there], za_send.at[s], za_recv.at[s],
                    h, flip(r, 1 << bits[s]))

    rounds = max(steps, len(partners))
    z_copy = None
    for i in range(rounds):
        h_copy = None
        if i < len(partners):
            h_copy = send(h_sum.at[i], h_in.at[i], h_send.at[i], h_recv.at[i], *partners[i])
        if i < steps:
            s = z_order[i]
            if z_copy is not None:
                z_copy.wait_recv()
                up = (r // (1 << bits[s + 1])) % 2
                z_start = z_start - length * up
                length = 2 * length
            z_copy = gather_step(s, z_start, length)
        if i == 1:
            @pl.when(jnp.logical_not(stays))
            def _():
                z_move.start()

            @pl.when(stays)
            def _():
                z_stay.start()
        if h_copy is not None:
            h_copy.wait_recv()
            h_sum[i + 1] = h_sum[i] + h_in[i]
    h_all[layer] = h_sum[len(partners)]
    h_copies = []
    for d in range(1, layers):
        mask = 0
        for t in range(layer_bits):
            mask |= ((d >> (layer_bits - 1 - t)) & 1) << bits[t]
        h_copies.append(send(h_all.at[layer], h_all.at[layer], ha_send.at[d], ha_recv.at[d],
                             h, flip(r, mask)))
    for copy in h_copies:
        copy.wait_recv()
    z_copy.wait_recv()

    for layer_id in range(layers):
        for b in range(2):
            result = None
            for c in range(chunks):
                at = pl.ds(c * piece, piece)
                z_bf = z_all[layer_id * chunks + c]
                term = fast(e_high[layer_id, b, :, at], z_bf, NT)
                term = term + fast(e_low[layer_id, b, :, at], z_bf, NT)
                result = term if result is None else result + term
            p_part[layer_id, b] = result
    p_copies = []
    for d in range(1, 2 * layers):
        to = flip(h, d // 2)
        p_copies.append(send(p_part.at[to, d % 2], p_in.at[d - 1], p_send.at[d], p_recv.at[d],
                             to, flip(r, 2 * (d % 2))))

    row_inv = inverse_factor(aug, h_all[h])
    z_stay.wait()
    right_ref[0] = math.sqrt(width) * exact(row_inv, z_recv[...]).T
    p_own = p_part[h, 0]
    for d in range(1, 2 * layers):
        p_copies[d - 1].wait_recv()
        p_own = p_own + p_in[d - 1]
    left_ref[0] = exact(p_own, row_inv, NT)[:n]

    for copy in pending:
        copy.wait_send()

    @pl.when(jnp.logical_not(stays))
    def _():
        z_move.wait_send()

    @pl.when(sends_s)
    def _():
        @pl.loop(0, devices // 2)
        def _(m):
            to, copy = s_copy(m)

            @pl.when(to != r)
            def _():
                copy.wait_send()

    out0.wait()
    out1.wait()


def shards(weights, sketch):
    _, n, width = weights.shape
    rank = sketch.shape[1]
    layers = lax.axis_size("layer")
    devices = lax.axis_size("rows")
    block = width // (2 * layers)
    chunks = devices // (2 * layers)
    piece = width // devices
    pad = -(-n // 16) * 16
    steps = devices.bit_length() - 2
    rounds = steps + 1
    group = 2 * layers
    dma = pltpu.SemaphoreType.DMA
    vmem = pltpu.VMEM
    small = (rank, rank)
    scratch = [
        vmem((layers, 2, n, block), BF16),
        vmem((layers, n, block), BF16),
        vmem((layers, 2, pad, block), BF16),
        vmem((layers, 2, pad, block), BF16),
        vmem((2, n, block), BF16),
        vmem((chunks, piece, rank), BF16),
        vmem((layers, 2, pad, rank), F32),
        vmem((group - 1, pad, rank), F32),
        vmem((layers, 2, pad, rank), F32),
        vmem((layers, 2, pad, rank), F32),
        vmem((group - 1, pad, rank), F32),
        vmem((steps + 1, *small), F32),
        vmem((steps, *small), F32),
        vmem((layers, *small), F32),
        vmem((layers * chunks, rank, piece), F32),
        vmem((layers * chunks, rank, piece), F32),
        vmem((rank, piece), F32),
        vmem((rank, piece), F32),
        vmem((layers * chunks, rank, piece), BF16),
        vmem((rounds + 1, *small), F32),
        vmem((rounds, *small), F32),
        vmem((layers, *small), F32),
        vmem((rank, 2 * rank), F32),
        dma((4,)),
        dma((2, layers)), dma((2, layers)), dma((layers,)), dma((layers,)),
        dma((devices // 2,)), dma((chunks,)),
        dma((group,)), dma((group,)), dma((group,)), dma((group,)), dma((group,)), dma((group,)),
        dma((steps,)), dma((steps,)), dma((layers,)), dma((layers,)), dma((steps,)), dma((steps,)),
        dma((rounds,)), dma((rounds,)), dma((layers,)), dma((layers,)),
        dma((steps,)), dma((steps,)), dma((1,)), dma((1,)),
    ]
    anywhere = pl.BlockSpec(memory_space=pl.ANY)
    on_chip = pl.BlockSpec(memory_space=pltpu.VMEM)
    return pl.pallas_call(
        functools.partial(kernel, layers, devices),
        out_shape=(
            jax.ShapeDtypeStruct((n, width // layers), BF16),
            jax.ShapeDtypeStruct((1, n, rank), F32),
            jax.ShapeDtypeStruct((1, n, rank), F32),
            jax.ShapeDtypeStruct((1, piece, rank), F32),
        ),
        in_specs=[anywhere, anywhere],
        out_specs=(anywhere, on_chip, on_chip, on_chip),
        scratch_shapes=scratch,
        compiler_params=pltpu.CompilerParams(
            collective_id=0, has_side_effects=True, vmem_limit_bytes=56 * 1024 * 1024
        ),
    )(weights, sketch)


def solution(mesh):
    return jax.shard_map(
        shards,
        mesh=mesh,
        in_specs=(P("layer", "rows", None), P("rows", None)),
        out_specs=(
            P("rows", "layer"),
            P("layer", "rows", None),
            P("layer", "rows", None),
            P("layer", "rows", None),
        ),
        check_vma=False,
    )
```

time: 474 us -> 179 us (0.38)
  the two profiles are of different devices: /device:TPU:0 before, /device:TPU:27 now
where the time goes in v1:
time: 179 us
  Pallas kernels  173 us (97%)
  local copies, waits for them, and re-layouts  5.03 us (3%)
    pallas_call x1, Pallas kernels, shards(): pl.pallas_call(functools.partial(kernel, layers, devices), out_shape=(jax...  173 us
    unnamed x10, local copies, waits for them, and re-layouts  5.03 us

profile of v1, /device:TPU:27, one launch (start us, length us, event | category | flops | bytes accessed | tf_op | source)
XLA Modules:
  0.0 178.6 jit_solution(6525706174375931688)
XLA Ops:
  0.6 172.9 %shard_map.57 = (bf16[232,4096]{1,0:T(8,128)(2,1)}, f32[1,232,128]{2,1,0:T(8,128)}, f32[1,232,128]{2,1,0:T(8,128)}, f32[1,512,128]{2,1,0:T(8,128)}) custom-call(bf16[1,232,8192]{2,1,0:T(8,128)(2,1)} %w_ref.1, bf16[512,128]{1,0:T(8,128)(2,1)} %sketch_ref.1), custom_call_target="tpu_custom_call" | custom-call | tf_op jit(solution)/shard_map/pallas_call | solution.py:472
  173.6 0.0 copy-start.2
  173.6 0.0 copy-start.1
  173.6 0.0 copy-start
  173.6 3.0 %copy.10 = bf16[232,4096]{1,0:T(8,128)(2,1)} copy(bf16[232,4096]{1,0:T(8,128)(2,1)} %get-tuple-element.8) | data formatting | bytes 3801088
  176.6 0.0 copy-done.2
  176.6 0.6 copy.11
  177.3 0.0 copy-done.1
  177.3 0.6 copy.12
  177.9 0.0 copy-done
  177.9 0.7 copy.13
Async XLA Ops:
  173.6 3.1 %copy-start.2 = (f32[1,232,128]{2,1,0:T(8,128)S(1)}, f32[1,232,128]{2,1,0:T(8,128)}, u32[]{:S(2)}) copy-start(f32[1,232,128]{2,1,0:T(8,128)} %get-tuple-element.9) | copy-start | bytes 356356
  173.6 3.7 %copy-start.1 = (f32[1,232,128]{2,1,0:T(8,128)S(1)}, f32[1,232,128]{2,1,0:T(8,128)}, u32[]{:S(2)}) copy-start(f32[1,232,128]{2,1,0:T(8,128)} %get-tuple-element.10) | copy-start | bytes 356356
  173.6 4.3 %copy-start = (f32[1,512,128]{2,1,0:T(8,128)S(1)}, f32[1,512,128]{2,1,0:T(8,128)}, u32[]{:S(2)}) copy-start(f32[1,512,128]{2,1,0:T(8,128)} %get-tuple-element.11) | copy-start | bytes 786436

commit v2 on v1

--- a/solution.py
+++ b/solution.py
@@ -13,6 +13,7 @@
 BF16 = jnp.bfloat16
 NN = (((1,), (0,)), ((), ()))
 NT = (((1,), (1,)), ((), ()))
+PIECES = 4
 
 
 def flip(value, mask):
@@ -40,12 +41,16 @@
     return high, (value - high.astype(F32)).astype(BF16)
 
 
-def inverse_factor(aug, gram):
+def begin_inverse(aug, gram):
     size = gram.shape[0]
     row_of = lax.broadcasted_iota(jnp.int32, (size, size), 0)
     col_of = lax.broadcasted_iota(jnp.int32, (size, size), 1)
     aug[:, :size] = gram
     aug[:, size:] = jnp.where(row_of == col_of, 1.0, 0.0).astype(F32)
+
+
+def eliminate(aug, first, stop):
+    size = aug.shape[0]
     row_id = lax.broadcasted_iota(jnp.int32, (size, 1), 0)
     lane_id = lax.broadcasted_iota(jnp.int32, (1, size), 1)
 
@@ -65,8 +70,7 @@
         aug[:, size:] = jnp.where(here, unit[:, size:], right - factor * unit[:, size:])
         return carry
 
-    lax.fori_loop(0, size, step, 0)
-    return aug[:, size:]
+    lax.fori_loop(first, stop, step, 0)
 
 
 def kernel(
@@ -121,19 +125,36 @@
     def columns(q):
         return pl.ds(pl.multiple_of(q * block, block), block)
 
-    far = []
-    near = []
     own_x = flip(r, 2)
-    for d in range(1, layers):
-        to = flip(h, d)
-        far.append(send(w_ref.at[0, :, columns(2 * to + (1 - x))], w_far.at[h],
-                        wy_send.at[0, d], wy_recv.at[0, d], to, r))
-    for d in range(1, layers):
-        to = flip(h, d)
-        near.append(send(w_ref.at[0, :, columns(2 * to + x)], w_in.at[h, 0],
-                         wy_send.at[1, d], wy_recv.at[1, d], to, r))
-    side = [send(w_ref.at[0, :, columns(2 * h + (1 - x))], w_in.at[h, 1],
-                 wx_send.at[0], wx_recv.at[0], h, own_x)]
+    part_width = block // PIECES
+
+    def part(q, p):
+        return pl.ds(pl.multiple_of(q * block + p * part_width, part_width), part_width)
+
+    def within(p):
+        return pl.ds(p * part_width, part_width)
+
+    def over_layers(i):
+        near, p = i // PIECES, i % PIECES
+        copies = []
+        for d in range(1, layers):
+            to = flip(h, d)
+            if near:
+                copies.append(send(w_ref.at[0, :, part(2 * to + x, p)], w_in.at[h, 0, :, within(p)],
+                                   wy_send.at[1, d, p], wy_recv.at[1, d, p], to, r))
+            else:
+                copies.append(send(w_ref.at[0, :, part(2 * to + (1 - x), p)],
+                                   w_far.at[h, :, within(p)],
+                                   wy_send.at[0, d, p], wy_recv.at[0, d, p], to, r))
+        return copies
+
+    def own_side(p):
+        return [send(w_ref.at[0, :, part(2 * h + (1 - x), p)], w_in.at[h, 1, :, within(p)],
+                     wx_send.at[0, p], wx_recv.at[0, p], h, own_x)]
+
+    ahead = 2
+    queue = [over_layers(i) for i in range(ahead)]
+    side = [own_side(p) for p in range(ahead)]
     mine0 = pltpu.make_async_copy(w_ref.at[0, :, columns(quarter)], w_in.at[h, 0], local_sem.at[0])
     mine1 = pltpu.make_async_copy(
         w_ref.at[0, :, columns(2 * h + (1 - x))], w_far.at[h], local_sem.at[1]
@@ -173,28 +194,20 @@
         e_high[:, :, low:, :] = zero
         e_low[:, :, low:, :] = zero
 
-    mine1.wait()
-    for d in range(1, layers):
-        far[d - 1].wait_recv()
-        from_layer = flip(h, d)
-        side.append(send(w_far.at[from_layer], w_in.at[from_layer, 1],
-                         wx_send.at[d], wx_recv.at[d], h, own_x))
-
     tile = 128
-
-    @pl.loop(0, block // tile)
-    def _(t):
-        at = pl.ds(pl.multiple_of(t * tile, tile), tile)
-        total_w = w_far[0, :, at].astype(F32)
-        for layer in range(1, layers):
-            total_w = total_w + w_far[layer, :, at].astype(F32)
-        base_v[1, :, at] = (total_w / layers).astype(BF16)
-
-    out1 = pltpu.make_async_copy(base_v.at[1], base_ref.at[:, columns(1 - x)], local_sem.at[2])
-    out1.start()
-
-    def residuals(b):
-        @pl.loop(0, block // tile)
+    inner = part_width // tile
+
+    def other_base(p):
+        @pl.loop(p * inner, (p + 1) * inner)
+        def _(t):
+            at = pl.ds(pl.multiple_of(t * tile, tile), tile)
+            total_w = w_far[0, :, at].astype(F32)
+            for layer in range(1, layers):
+                total_w = total_w + w_far[layer, :, at].astype(F32)
+            base_v[1, :, at] = (total_w / layers).astype(BF16)
+
+    def residuals(b, p):
+        @pl.loop(p * inner, (p + 1) * inner)
         def _(t):
             at = pl.ds(pl.multiple_of(t * tile, tile), tile)
             total_w = w_in[0, b, :, at].astype(F32)
@@ -209,24 +222,49 @@
                 e_high[layer, b, :n, at] = high
                 e_low[layer, b, :n, at] = low
 
-    def sampled(b):
-        sketch = s_v[...].reshape(block, s_v.shape[2])
+    def sampled(b, p):
+        per = chunks // PIECES
+        sketch = s_v[p * per:(p + 1) * per].reshape(part_width, s_v.shape[2])
         for layer in range(layers):
-            y_part[layer, b] = fast(e_high[layer, b], sketch) + fast(e_low[layer, b], sketch)
-
-    mine0.wait()
-    for copy in near:
-        copy.wait_recv()
-    residuals(0)
+            term = fast(e_high[layer, b, :, within(p)], sketch)
+            term = term + fast(e_low[layer, b, :, within(p)], sketch)
+            if p == 0:
+                y_part[layer, b] = term
+            else:
+                y_part[layer, b] = y_part[layer, b] + term
+
+    mine1.wait()
+    for i in range(2 * PIECES):
+        near, p = i // PIECES, i % PIECES
+        for copy in queue[i]:
+            copy.wait_recv()
+        if i + ahead < 2 * PIECES:
+            queue.append(over_layers(i + ahead))
+        if not near:
+            for d in range(1, layers):
+                source = flip(h, d)
+                side[p].append(send(w_far.at[source, :, within(p)], w_in.at[source, 1, :, within(p)],
+                                    wx_send.at[d, p], wx_recv.at[d, p], h, own_x))
+            if p + ahead < PIECES:
+                side.append(own_side(p + ahead))
+            other_base(p)
+            if p == PIECES - 1:
+                out1 = pltpu.make_async_copy(
+                    base_v.at[1], base_ref.at[:, columns(1 - x)], local_sem.at[2]
+                )
+                out1.start()
+                mine0.wait()
+                for c in range(chunks):
+                    pltpu.make_async_copy(sketch_ref, s_v.at[c], s_recv.at[c]).wait()
+        else:
+            residuals(0, p)
+            sampled(0, p)
+            for copy in side[p]:
+                copy.wait_recv()
+            residuals(1, p)
+            sampled(1, p)
     out0 = pltpu.make_async_copy(base_v.at[0], base_ref.at[:, columns(x)], local_sem.at[3])
     out0.start()
-    for c in range(chunks):
-        pltpu.make_async_copy(sketch_ref, s_v.at[c], s_recv.at[c]).wait()
-    sampled(0)
-    for copy in side:
-        copy.wait_recv()
-    residuals(1)
-    sampled(1)
 
     def to_owner(part, slots, ss, rs):
         copies = []
@@ -246,39 +284,40 @@
     for d in range(1, 2 * layers):
         copies.append(send(y_all.at[h, 0], y_all.at[h, d % 2], ya_send.at[d], ya_recv.at[d],
                            flip(h, d // 2), flip(r, 2 * (d % 2))))
-    for copy in copies:
-        copy.wait_recv()
-
-    def turned(b, layer):
-        return y_all[layer, b].T
 
     def butterfly(total_ref, slots, ss, rs, partners):
         for i, (to_h, to_r) in enumerate(partners):
             copy = send(total_ref.at[i], slots.at[i], ss.at[i], rs.at[i], to_h, to_r)
+            yield
             copy.wait_recv()
             total_ref[i + 1] = total_ref[i] + slots[i]
-        return total_ref[len(partners)]
-
-    gram[0] = exact(turned(0, h), y_all[h, 0]) + exact(turned(1, h), y_all[h, 1])
-    g_total = [None]
-
+
+    gram[0] = exact(y_own.T, y_own)
+    gram_sum = butterfly(gram, gram_in, g_send, g_recv,
+                         [(h, flip(r, 1 << bit)) for bit in range(row_bits)])
+    next(gram_sum)
     piece = width // devices
-    for layer in range(layers):
-        both = None
-        for b in range(2):
-            high, low = split(turned(b, layer))
-            term = (
-                fast(high, e_high[layer, b]) + fast(low, e_high[layer, b])
-                + fast(high, e_low[layer, b])
-            )
-            both = term if both is None else both + term
+    for d in range(2 * layers):
+        if d > 0:
+            copies[d - 1].wait_recv()
+        layer, b = flip(h, d // 2), d % 2
+        high, low = split(y_all[layer, b].T)
         for c in range(chunks):
-            w_sum[layer * chunks + c] = both[:, c * piece:(c + 1) * piece]
-
+            at = pl.ds(c * piece, piece)
+            e_part = e_high[layer, b, :, at]
+            term = fast(high, e_part) + fast(low, e_part) + fast(high, e_low[layer, b, :, at])
+            if b == 0:
+                w_sum[layer * chunks + c] = term
+            else:
+                w_sum[layer * chunks + c] = w_sum[layer * chunks + c] + term
+        if d < 2 * layers - 1:
+            next(gram_sum, None)
+
+    rank = gram.shape[1]
     start = 0
     offset = 0
     length = layers * chunks
-    scatter = []
+    done = 0
     for s, bit in enumerate(bits):
         half = length // 2
         up = (r // (1 << bit)) % 2
@@ -286,18 +325,21 @@
         give = start + half * (1 - up)
         w_copy = send(w_sum.at[pl.ds(give, half)], w_half.at[pl.ds(offset, half)],
                       ws_send.at[s], ws_recv.at[s], h, flip(r, 1 << bit))
-        g_copy = send(gram.at[s], gram_in.at[s], g_send.at[s], g_recv.at[s], h, flip(r, 1 << bit))
-        g_copy.wait_recv()
-        gram[s + 1] = gram[s] + gram_in[s]
+        if s == 0:
+            for _ in gram_sum:
+                pass
+            begin_inverse(aug, gram[row_bits])
+        stop = rank // 6 + (rank - rank // 6) * s // (steps - 1)
+        eliminate(aug, done, stop)
+        done = stop
         if s == steps - 1:
-            inv[h] = inverse_factor(aug, gram[s + 1])
+            inv[h] = aug[:, rank:]
             l_copies = [
                 send(inv.at[h], inv.at[h], l_send.at[d], l_recv.at[d], flip(h, d), r)
                 for d in range(1, layers)
             ]
             basis_ref[0] = exact(y_all[h, 0], inv[h], NT)[:n]
         w_copy.wait_recv()
-
         for i in range(half):
             w_sum[keep + i] = w_sum[keep + i] + w_half[offset + i]
         start = keep
@@ -323,45 +365,28 @@
     z_stay = pltpu.make_async_copy(z_own, z_recv, zf_recv.at[0])
 
     partners = [(h, flip(r, 2))]
+    partners += [(flip(h, 1 << i), r) for i in range(layer_bits)]
     partners += [(h, flip(r, 1 << bit)) for bit in bits[layer_bits:]]
-    partners += [(flip(h, 1 << i), r) for i in range(layer_bits)]
-    gather_at = [start]
-    length = 1
-    last = None
-    z_order = list(range(steps))[::-1]
-    z_copies = [None] * steps
-    z_start = start
-
-    def gather_step(s, z_start, length):
-        there = pl.ds(z_start, length)
-        return send(z_all.at[there], z_all.at[there], za_send.at[s], za_recv.at[s],
-                    h, flip(r, 1 << bits[s]))
-
-    rounds = max(steps, len(partners))
-    z_copy = None
-    for i in range(rounds):
-        h_copy = None
-        if i < len(partners):
-            h_copy = send(h_sum.at[i], h_in.at[i], h_send.at[i], h_recv.at[i], *partners[i])
-        if i < steps:
-            s = z_order[i]
-            if z_copy is not None:
-                z_copy.wait_recv()
-                up = (r // (1 << bits[s + 1])) % 2
-                z_start = z_start - length * up
-                length = 2 * length
-            z_copy = gather_step(s, z_start, length)
-        if i == 1:
-            @pl.when(jnp.logical_not(stays))
-            def _():
-                z_move.start()
-
-            @pl.when(stays)
-            def _():
-                z_stay.start()
-        if h_copy is not None:
-            h_copy.wait_recv()
-            h_sum[i + 1] = h_sum[i] + h_in[i]
+    h_part = butterfly(h_sum, h_in, h_send, h_recv, partners)
+
+    def gather(z_start):
+        length = 1
+        for s in reversed(range(steps)):
+            there = pl.ds(z_start, length)
+            copy = send(z_all.at[there], z_all.at[there], za_send.at[s], za_recv.at[s],
+                        h, flip(r, 1 << bits[s]))
+            yield
+            copy.wait_recv()
+            z_start = z_start - length * ((r // (1 << bits[s])) % 2)
+            length = 2 * length
+
+    z_gather = gather(start)
+    next(h_part)
+    next(z_gather)
+    for i in range(len(partners)):
+        next(h_part, None)
+        if i == len(partners) - 2:
+            next(z_gather, None)
     h_all[layer] = h_sum[len(partners)]
     h_copies = []
     for d in range(1, layers):
@@ -370,9 +395,23 @@
             mask |= ((d >> (layer_bits - 1 - t)) & 1) << bits[t]
         h_copies.append(send(h_all.at[layer], h_all.at[layer], ha_send.at[d], ha_recv.at[d],
                              h, flip(r, mask)))
+
+    @pl.when(jnp.logical_not(stays))
+    def _():
+        z_move.start()
+
+    @pl.when(stays)
+    def _():
+        z_stay.start()
+
     for copy in h_copies:
         copy.wait_recv()
-    z_copy.wait_recv()
+    begin_inverse(aug, h_all[h])
+    eliminate(aug, 0, rank // 8)
+    next(z_gather, None)
+    eliminate(aug, rank // 8, rank // 4)
+    for _ in z_gather:
+        pass
 
     for layer_id in range(layers):
         for b in range(2):
@@ -390,7 +429,8 @@
         p_copies.append(send(p_part.at[to, d % 2], p_in.at[d - 1], p_send.at[d], p_recv.at[d],
                              to, flip(r, 2 * (d % 2))))
 
-    row_inv = inverse_factor(aug, h_all[h])
+    eliminate(aug, rank // 4, rank)
+    row_inv = aug[:, rank:]
     z_stay.wait()
     right_ref[0] = math.sqrt(width) * exact(row_inv, z_recv[...]).T
     p_own = p_part[h, 0]
@@ -447,8 +487,8 @@
         vmem((layers, 2, pad, rank), F32),
         vmem((layers, 2, pad, rank), F32),
         vmem((group - 1, pad, rank), F32),
-        vmem((steps + 1, *small), F32),
-        vmem((steps, *small), F32),
+        vmem((rounds + 1, *small), F32),
+        vmem((rounds, *small), F32),
         vmem((layers, *small), F32),
         vmem((layers * chunks, rank, piece), F32),
         vmem((layers * chunks, rank, piece), F32),
@@ -460,10 +500,10 @@
         vmem((layers, *small), F32),
         vmem((rank, 2 * rank), F32),
         dma((4,)),
-        dma((2, layers)), dma((2, layers)), dma((layers,)), dma((layers,)),
+        dma((2, layers, PIECES)), dma((2, layers, PIECES)), dma((layers, PIECES)), dma((layers, PIECES)),
         dma((devices // 2,)), dma((chunks,)),
         dma((group,)), dma((group,)), dma((group,)), dma((group,)), dma((group,)), dma((group,)),
-        dma((steps,)), dma((steps,)), dma((layers,)), dma((layers,)), dma((steps,)), dma((steps,)),
+        dma((rounds,)), dma((rounds,)), dma((layers,)), dma((layers,)), dma((steps,)), dma((steps,)),
         dma((rounds,)), dma((rounds,)), dma((layers,)), dma((layers,)),
         dma((steps,)), dma((steps,)), dma((1,)), dma((1,)),
     ]

time: 179 us -> 155 us (0.87)
  the two profiles are of different devices: /device:TPU:27 before, /device:TPU:0 now
where the time goes in v2:
time: 155 us; the launch traced here: 154 us
  Pallas kernels  149 us (96%)
  local copies, waits for them, and re-layouts  5.03 us (3%)
    pallas_call x1, Pallas kernels, shards(): pl.pallas_call(functools.partial(kernel, layers, devices), out_shape=(jax...  149 us
    unnamed x10, local copies, waits for them, and re-layouts  5.03 us

profile of v2, /device:TPU:0, one launch (start us, length us, event | category | flops | bytes accessed | tf_op | source)
XLA Modules:
  0.0 154.4 jit_solution(1318744850571651288)
XLA Ops:
  0.6 148.7 %shard_map.57 = (bf16[232,4096]{1,0:T(8,128)(2,1)}, f32[1,232,128]{2,1,0:T(8,128)}, f32[1,232,128]{2,1,0:T(8,128)}, f32[1,512,128]{2,1,0:T(8,128)}) custom-call(bf16[1,232,8192]{2,1,0:T(8,128)(2,1)} %w_ref.1, bf16[512,128]{1,0:T(8,128)(2,1)} %sketch_ref.1), custom_call_target="tpu_custom_call" | custom-call | tf_op jit(solution)/shard_map/pallas_call | solution.py:512
  149.3 0.0 copy-start.2
  149.3 0.0 copy-start.1
  149.3 0.0 copy-start
  149.3 3.0 %copy.10 = bf16[232,4096]{1,0:T(8,128)(2,1)} copy(bf16[232,4096]{1,0:T(8,128)(2,1)} %get-tuple-element.8) | data formatting | bytes 3801088
  152.4 0.0 copy-done.2
  152.4 0.6 copy.11
  153.0 0.0 copy-done.1
  153.0 0.6 copy.12
  153.7 0.0 copy-done
  153.7 0.7 copy.13
Async XLA Ops:
  149.3 3.1 %copy-start.2 = (f32[1,232,128]{2,1,0:T(8,128)S(1)}, f32[1,232,128]{2,1,0:T(8,128)}, u32[]{:S(2)}) copy-start(f32[1,232,128]{2,1,0:T(8,128)} %get-tuple-element.9) | copy-start | bytes 356356
  149.3 3.7 %copy-start.1 = (f32[1,232,128]{2,1,0:T(8,128)S(1)}, f32[1,232,128]{2,1,0:T(8,128)}, u32[]{:S(2)}) copy-start(f32[1,232,128]{2,1,0:T(8,128)} %get-tuple-element.10) | copy-start | bytes 356356
  149.3 4.3 %copy-start = (f32[1,512,128]{2,1,0:T(8,128)S(1)}, f32[1,512,128]{2,1,0:T(8,128)}, u32[]{:S(2)}) copy-start(f32[1,512,128]{2,1,0:T(8,128)} %get-tuple-element.11) | copy-start | bytes 786436

commit v3 on v2

--- a/solution.py
+++ b/solution.py
@@ -54,23 +54,40 @@
     row_id = lax.broadcasted_iota(jnp.int32, (size, 1), 0)
     lane_id = lax.broadcasted_iota(jnp.int32, (1, size), 1)
 
-    def step(k, carry):
-        row = aug[pl.ds(k, 1), :]
+    def root(pivot):
+        scale = lax.rsqrt(pivot)
+        return scale * (1.5 - 0.5 * (pivot * scale) * scale)
+
+    def pick(rows, hot):
+        return jnp.sum(jnp.where(hot, rows, 0.0), axis=1, keepdims=True)
+
+    def step(pair, carry):
+        k = 2 * pair
+        row_a = aug[pl.ds(k, 1), :]
+        row_b = aug[pl.ds(k + 1, 1), :]
         left = aug[:, :size]
         right = aug[:, size:]
-        hot = lane_id == k
-        pivot = jnp.sum(jnp.where(hot, row[:, :size], 0.0), axis=1, keepdims=True)
-        scale = lax.rsqrt(pivot)
-        scale = scale * (1.5 - 0.5 * (pivot * scale) * scale)
-        column = jnp.sum(jnp.where(hot, left, 0.0), axis=1, keepdims=True)
-        unit = row * scale
-        factor = jnp.where(row_id > k, column * scale, 0.0)
-        here = row_id == k
-        aug[:, :size] = jnp.where(here, unit[:, :size], left - factor * unit[:, :size])
-        aug[:, size:] = jnp.where(here, unit[:, size:], right - factor * unit[:, size:])
+        hot_a = lane_id == k
+        hot_b = lane_id == k + 1
+        cross = pick(row_a[:, :size], hot_b)
+        scale_a = root(pick(row_a[:, :size], hot_a))
+        corner = pick(row_b[:, :size], hot_b)
+        col_a = pick(left, hot_a)
+        col_b = pick(left, hot_b)
+        slope = cross * scale_a
+        scale_b = root(corner - slope * slope)
+        unit_a = row_a * scale_a
+        unit_b = (row_b - slope * unit_a) * scale_b
+        factor_a = col_a * scale_a
+        factor_b = jnp.where(row_id > k + 1, (col_b - slope * factor_a) * scale_b, 0.0)
+        factor_a = jnp.where(row_id > k + 1, factor_a, 0.0)
+        for at, old in ((slice(0, size), left), (slice(size, 2 * size), right)):
+            new = old - factor_a * unit_a[:, at] - factor_b * unit_b[:, at]
+            new = jnp.where(row_id == k, unit_a[:, at], new)
+            aug[:, at] = jnp.where(row_id == k + 1, unit_b[:, at], new)
         return carry
 
-    lax.fori_loop(first, stop, step, 0)
+    lax.fori_loop(first // 2, stop // 2, step, 0)
 
 
 def kernel(
@@ -110,17 +127,38 @@
         return copy
 
     barrier = pltpu.get_barrier_semaphore()
-    total = layers * devices
     me = h * devices + r
 
-    @pl.loop(1, total)
-    def _(i):
-        other = lax.rem(me + i, total)
-        pl.semaphore_signal(
-            barrier, inc=1, device_id=(other // devices, other % devices), device_id_type=MESH
-        )
-
-    pl.semaphore_wait(barrier, total - 1)
+    def greet(to_h, to_r):
+        pl.semaphore_signal(barrier, inc=1, device_id=(to_h, to_r), device_id_type=MESH)
+
+    for d in range(1, 2 * layers):
+        greet(flip(h, d // 2), flip(r, 2 * (d % 2)))
+
+    @pl.loop(0, devices // 2)
+    def _(m):
+        to = (m // 2) * 4 + x * 2 + m % 2
+
+        @pl.when(to != r)
+        def _():
+            greet(h, to)
+
+    giver_quarter = r // chunks
+    giver_chunk = h * chunks + r % chunks
+    giver_h = giver_quarter // 2
+    giver_r = 2 * (giver_quarter % 2)
+    for s, bit in enumerate(bits):
+        giver_r = giver_r + (1 << bit) * ((giver_chunk // (1 << (steps - 1 - s))) % 2)
+    gets_own = giver_h * devices + giver_r == me
+
+    @pl.when(jnp.logical_not(gets_own))
+    def _():
+        greet(giver_h, giver_r)
+        pl.semaphore_wait(barrier, 2 * layers - 1 + devices // 2)
+
+    @pl.when(gets_own)
+    def _():
+        pl.semaphore_wait(barrier, 2 * layers - 1 + devices // 2 - 1)
 
     def columns(q):
         return pl.ds(pl.multiple_of(q * block, block), block)
@@ -164,28 +202,42 @@
 
     s_quarter = r // chunks
     s_slot = r % chunks
-    sends_s = (s_quarter // 2) == h
-
-    def s_copy(m):
-        to = (m // 2) * 4 + (s_quarter % 2) * 2 + m % 2
+    in_plane = (s_quarter // 2) == h
+    is_root = jnp.logical_and(in_plane, (s_quarter % 2) == x)
+    crosses = jnp.logical_and(in_plane, (s_quarter % 2) != x)
+    other_slot = flip(r, 2) % chunks
+    cross_copy = pltpu.make_async_remote_copy(
+        src_ref=sketch_ref, dst_ref=s_v.at[s_slot], send_sem=s_send.at[0, 0],
+        recv_sem=s_recv.at[s_slot], device_id=(h, own_x), device_id_type=MESH,
+    )
+    s_stay = pltpu.make_async_copy(sketch_ref, s_v.at[s_slot], s_recv.at[s_slot])
+
+    def s_copy(m, which):
+        to = (m // 2) * 4 + x * 2 + m % 2
+        slot = other_slot if which else s_slot
         return to, pltpu.make_async_remote_copy(
-            src_ref=sketch_ref, dst_ref=s_v.at[s_slot], send_sem=s_send.at[m],
-            recv_sem=s_recv.at[s_slot], device_id=(h, to), device_id_type=MESH,
+            src_ref=s_v.at[slot] if which else sketch_ref, dst_ref=s_v.at[slot],
+            send_sem=s_send.at[which, m],
+            recv_sem=s_recv.at[slot], device_id=(h, to), device_id_type=MESH,
         )
 
-    @pl.when(sends_s)
-    def _():
+    def spread(which, action):
         @pl.loop(0, devices // 2)
         def _(m):
-            to, copy = s_copy(m)
+            to, copy = s_copy(m, which)
 
             @pl.when(to != r)
             def _():
-                copy.start()
-
-            @pl.when(to == r)
-            def _():
-                pltpu.make_async_copy(sketch_ref, s_v.at[s_slot], s_recv.at[s_slot]).start()
+                action(copy)
+
+    @pl.when(crosses)
+    def _():
+        cross_copy.start()
+
+    @pl.when(is_root)
+    def _():
+        s_stay.start()
+        spread(0, lambda copy: copy.start())
 
     pad = e_high.shape[2]
     if pad > n:
@@ -232,6 +284,11 @@
                 y_part[layer, b] = term
             else:
                 y_part[layer, b] = y_part[layer, b] + term
+
+    @pl.when(is_root)
+    def _():
+        pltpu.make_async_copy(sketch_ref, s_v.at[other_slot], s_recv.at[other_slot]).wait()
+        spread(1, lambda copy: copy.start())
 
     mine1.wait()
     for i in range(2 * PIECES):
@@ -255,7 +312,9 @@
                 out1.start()
                 mine0.wait()
                 for c in range(chunks):
-                    pltpu.make_async_copy(sketch_ref, s_v.at[c], s_recv.at[c]).wait()
+                    @pl.when(jnp.logical_not(jnp.logical_and(is_root, other_slot == c)))
+                    def _():
+                        pltpu.make_async_copy(sketch_ref, s_v.at[c], s_recv.at[c]).wait()
         else:
             residuals(0, p)
             sampled(0, p)
@@ -329,7 +388,7 @@
             for _ in gram_sum:
                 pass
             begin_inverse(aug, gram[row_bits])
-        stop = rank // 6 + (rank - rank // 6) * s // (steps - 1)
+        stop = (rank // 6 + (rank - rank // 6) * s // (steps - 1)) // 2 * 2
         eliminate(aug, done, stop)
         done = stop
         if s == steps - 1:
@@ -446,15 +505,14 @@
     def _():
         z_move.wait_send()
 
-    @pl.when(sends_s)
-    def _():
-        @pl.loop(0, devices // 2)
-        def _(m):
-            to, copy = s_copy(m)
-
-            @pl.when(to != r)
-            def _():
-                copy.wait_send()
+    @pl.when(crosses)
+    def _():
+        cross_copy.wait_send()
+
+    @pl.when(is_root)
+    def _():
+        spread(0, lambda copy: copy.wait_send())
+        spread(1, lambda copy: copy.wait_send())
 
     out0.wait()
     out1.wait()
@@ -501,7 +559,7 @@
         vmem((rank, 2 * rank), F32),
         dma((4,)),
         dma((2, layers, PIECES)), dma((2, layers, PIECES)), dma((layers, PIECES)), dma((layers, PIECES)),
-        dma((devices // 2,)), dma((chunks,)),
+        dma((2, devices // 2)), dma((chunks,)),
         dma((group,)), dma((group,)), dma((group,)), dma((group,)), dma((group,)), dma((group,)),
         dma((rounds,)), dma((rounds,)), dma((layers,)), dma((layers,)), dma((steps,)), dma((steps,)),
         dma((rounds,)), dma((rounds,)), dma((layers,)), dma((layers,)),

time: 155 us -> 152 us (0.981)
  Pallas kernels: 149 us -> 146 us
    pallas_call x1, Pallas kernels: 149 us -> 146 us  [shards(): pl.pallas_call(functools.partial(kernel, layers, devices), out_shape=(jax...]
where the time goes in v3:
time: 152 us; the launch traced here: 151 us
  Pallas kernels  146 us (96%)
  local copies, waits for them, and re-layouts  5.03 us (3%)
    pallas_call x1, Pallas kernels, shards(): pl.pallas_call(functools.partial(kernel, layers, devices), out_shape=(jax...  146 us
    unnamed x10, local copies, waits for them, and re-layouts  5.03 us

profile of v3, /device:TPU:0, one launch (start us, length us, event | category | flops | bytes accessed | tf_op | source)
XLA Modules:
  0.0 151.3 jit_solution(10630061951448076055)
XLA Ops:
  0.6 145.6 %shard_map.57 = (bf16[232,4096]{1,0:T(8,128)(2,1)}, f32[1,232,128]{2,1,0:T(8,128)}, f32[1,232,128]{2,1,0:T(8,128)}, f32[1,512,128]{2,1,0:T(8,128)}) custom-call(bf16[1,232,8192]{2,1,0:T(8,128)(2,1)} %w_ref.1, bf16[512,128]{1,0:T(8,128)(2,1)} %sketch_ref.1), custom_call_target="tpu_custom_call" | custom-call | tf_op jit(solution)/shard_map/pallas_call | solution.py:570
  146.3 0.0 copy-start.2
  146.3 0.0 copy-start.1
  146.3 0.0 copy-start
  146.3 3.0 %copy.10 = bf16[232,4096]{1,0:T(8,128)(2,1)} copy(bf16[232,4096]{1,0:T(8,128)(2,1)} %get-tuple-element.8) | data formatting | bytes 3801088
  149.3 0.0 copy-done.2
  149.3 0.6 copy.11
  150.0 0.0 copy-done.1
  150.0 0.6 copy.12
  150.6 0.0 copy-done
  150.6 0.7 copy.13
Async XLA Ops:
  146.3 3.1 %copy-start.2 = (f32[1,232,128]{2,1,0:T(8,128)S(1)}, f32[1,232,128]{2,1,0:T(8,128)}, u32[]{:S(2)}) copy-start(f32[1,232,128]{2,1,0:T(8,128)} %get-tuple-element.9) | copy-start | bytes 356356
  146.3 3.7 %copy-start.1 = (f32[1,232,128]{2,1,0:T(8,128)S(1)}, f32[1,232,128]{2,1,0:T(8,128)}, u32[]{:S(2)}) copy-start(f32[1,232,128]{2,1,0:T(8,128)} %get-tuple-element.10) | copy-start | bytes 356356
  146.3 4.3 %copy-start = (f32[1,512,128]{2,1,0:T(8,128)S(1)}, f32[1,512,128]{2,1,0:T(8,128)}, u32[]{:S(2)}) copy-start(f32[1,512,128]{2,1,0:T(8,128)} %get-tuple-element.11) | copy-start | bytes 786436

commit v4 on v3

--- a/solution.py
+++ b/solution.py
@@ -355,16 +355,19 @@
     gram_sum = butterfly(gram, gram_in, g_send, g_recv,
                          [(h, flip(r, 1 << bit)) for bit in range(row_bits)])
     next(gram_sum)
+    rank = gram.shape[1]
     piece = width // devices
     for d in range(2 * layers):
         if d > 0:
             copies[d - 1].wait_recv()
         layer, b = flip(h, d // 2), d % 2
         high, low = split(y_all[layer, b].T)
+        stacked = jnp.concatenate([high, low], axis=0)
         for c in range(chunks):
             at = pl.ds(c * piece, piece)
             e_part = e_high[layer, b, :, at]
-            term = fast(high, e_part) + fast(low, e_part) + fast(high, e_low[layer, b, :, at])
+            both = fast(stacked, e_part)
+            term = both[:rank] + both[rank:] + fast(high, e_low[layer, b, :, at])
             if b == 0:
                 w_sum[layer * chunks + c] = term
             else:
@@ -372,7 +375,6 @@
         if d < 2 * layers - 1:
             next(gram_sum, None)
 
-    rank = gram.shape[1]
     start = 0
     offset = 0
     length = layers * chunks
@@ -473,15 +475,14 @@
         pass
 
     for layer_id in range(layers):
-        for b in range(2):
-            result = None
-            for c in range(chunks):
-                at = pl.ds(c * piece, piece)
-                z_bf = z_all[layer_id * chunks + c]
-                term = fast(e_high[layer_id, b, :, at], z_bf, NT)
-                term = term + fast(e_low[layer_id, b, :, at], z_bf, NT)
-                result = term if result is None else result + term
-            p_part[layer_id, b] = result
+        result = None
+        for c in range(chunks):
+            at = pl.ds(c * piece, piece)
+            z_bf = z_all[layer_id * chunks + c]
+            term = fast(e_high[layer_id, :, :, at].reshape(2 * pad, piece), z_bf, NT)
+            term = term + fast(e_low[layer_id, :, :, at].reshape(2 * pad, piece), z_bf, NT)
+            result = term if result is None else result + term
+        p_part[layer_id] = result.reshape(2, pad, rank)
     p_copies = []
     for d in range(1, 2 * layers):
         to = flip(h, d // 2)

time: 152 us -> 152 us (level)
  no operation moved by 1% of the time
where the time goes in v4:
time: 152 us; the launch traced here: 151 us
  Pallas kernels  146 us (96%)
  local copies, waits for them, and re-layouts  5.03 us (3%)
    pallas_call x1, Pallas kernels, shards(): pl.pallas_call(functools.partial(kernel, layers, devices), out_shape=(jax...  146 us
    unnamed x10, local copies, waits for them, and re-layouts  5.03 us

profile of v4, /device:TPU:0, one launch (start us, length us, event | category | flops | bytes accessed | tf_op | source)
XLA Modules:
  0.0 151.4 jit_solution(5835294832635617049)
XLA Ops:
  0.6 145.7 %shard_map.57 = (bf16[232,4096]{1,0:T(8,128)(2,1)}, f32[1,232,128]{2,1,0:T(8,128)}, f32[1,232,128]{2,1,0:T(8,128)}, f32[1,512,128]{2,1,0:T(8,128)}) custom-call(bf16[1,232,8192]{2,1,0:T(8,128)(2,1)} %w_ref.1, bf16[512,128]{1,0:T(8,128)(2,1)} %sketch_ref.1), custom_call_target="tpu_custom_call" | custom-call | tf_op jit(solution)/shard_map/pallas_call | solution.py:571
  146.4 0.0 copy-start.2
  146.4 0.0 copy-start.1
  146.4 0.0 copy-start
  146.4 3.0 %copy.10 = bf16[232,4096]{1,0:T(8,128)(2,1)} copy(bf16[232,4096]{1,0:T(8,128)(2,1)} %get-tuple-element.8) | data formatting | bytes 3801088
  149.4 0.0 copy-done.2
  149.4 0.6 copy.11
  150.1 0.0 copy-done.1
  150.1 0.6 copy.12
  150.7 0.0 copy-done
  150.7 0.7 copy.13
Async XLA Ops:
  146.4 3.1 %copy-start.2 = (f32[1,232,128]{2,1,0:T(8,128)S(1)}, f32[1,232,128]{2,1,0:T(8,128)}, u32[]{:S(2)}) copy-start(f32[1,232,128]{2,1,0:T(8,128)} %get-tuple-element.9) | copy-start | bytes 356356
  146.4 3.7 %copy-start.1 = (f32[1,232,128]{2,1,0:T(8,128)S(1)}, f32[1,232,128]{2,1,0:T(8,128)}, u32[]{:S(2)}) copy-start(f32[1,232,128]{2,1,0:T(8,128)} %get-tuple-element.10) | copy-start | bytes 356356
  146.4 4.3 %copy-start = (f32[1,512,128]{2,1,0:T(8,128)S(1)}, f32[1,512,128]{2,1,0:T(8,128)}, u32[]{:S(2)}) copy-start(f32[1,512,128]{2,1,0:T(8,128)} %get-tuple-element.11) | copy-start | bytes 786436
